TPU v7x, 512 devices: a whole 4x8x8 slice. The times are simulated.
512 devices in a mesh: slab: 64 (over x, z, core), filt: 8 (over y).
Axes of the slice: x: 4, y: 8, z: 8, core: 2. Of those that a mesh axis runs over, the one named last changes fastest.
Arguments:
- volume: bfloat16 [128, 128, 16, 256], P('slab', 'filt'), may hold values from -6 to 6
- weights: bfloat16 [3, 3, 3, 128, 256], replicated, may hold values from -0.109375 to 0.109375
- out_error: bfloat16 [64, 256, 8, 128], P('slab', 'filt'), may hold values from -6 to 6
Outputs:
- in_grad: bfloat16 [128, 128, 16, 256], P('slab', None, 'filt')
- weight_grad: float32 [3, 3, 3, 128, 256], P(None, None, None, None, 'filt')
All inputs are finite; a program needn't handle non-finite values.
Results may differ from a plain program's by a relative error of at most 0.0049.
Values may be sent and summed in bfloat16 or wider, within the bound.
No kernel may reach another device: no remote copies, remote signals or barrier semaphores. Data moves between devices by JAX's collectives and lax.ppermute only.
A program may use at most 64 MiB of HBM per device.

v0:
```python
import math
import jax
import jax.numpy as jnp
from jax import lax
from jax.sharding import PartitionSpec as P


def shifted_2(value, axis, steps):
    count = lax.axis_size(axis)
    first, last = (max(0, -steps), min(count, count - steps))
    return lax.ppermute(value, axis, [(source, source + steps) for source in range(first, last)])


def tap_pieces(extended, top):
    depth = (extended.shape[0] - 1) // 2
    rows = (extended.shape[2] + top - 1) // 2
    cols = extended.shape[3] // 2
    chans = extended.shape[1]
    padded = jnp.pad(extended, ((0, 1), (0, 0), (top, 1), (1, 1)))
    split = padded.reshape(depth + 1, 2, chans, rows + 1, 2, cols + 1, 2)
    pieces = []
    for a in range(3):
        for b in range(3):
            for c in range(3):
                piece = split[
                    a // 2 : a // 2 + depth,
                    a % 2,
                    :,
                    b // 2 : b // 2 + rows,
                    b % 2,
                    c // 2 : c // 2 + cols,
                    c % 2,
                ]
                pieces.append(((a, b, c), piece))
    return pieces


def forward_taps(pieces, kernel):
    total = None
    for (a, b, c), piece in pieces:
        term = jnp.einsum(
            "dkhw,kf->dfhw", piece, kernel[a, b, c], preferred_element_type=jnp.float32
        )
        total = term if total is None else total + term
    return total


def weight_taps(pieces, grad):
    terms = []
    for (a, b, c), piece in pieces:
        terms.append(jnp.einsum("dkhw,dfhw->kf", piece, grad, preferred_element_type=jnp.float32))
    stacked = jnp.stack(terms, 0)
    return stacked.reshape((3, 3, 3) + stacked.shape[1:])


def input_taps(grad_ext, kernel):
    depth = grad_ext.shape[0] - 1
    rows = grad_ext.shape[2] - 1
    cols = grad_ext.shape[3]
    chans = kernel.shape[3]
    parity_taps = ((1,), (2, 0))
    shifted = {}
    for a in range(3):
        for b in range(3):
            for c in range(3):
                term = jnp.einsum(
                    "dfhw,kf->dkhw", grad_ext, kernel[a, b, c], preferred_element_type=jnp.float32
                )
                start_d = 1 if a == 0 else 0
                start_r = 1 if b == 0 else 0
                term = term[start_d : start_d + depth, :, start_r : start_r + rows]
                if c == 0:
                    term = jnp.pad(term[..., 1:], ((0, 0), (0, 0), (0, 0), (0, 1)))
                shifted[a, b, c] = term
    depth_parts = []
    for even_d in range(2):
        row_parts = []
        for even_r in range(2):
            col_parts = []
            for even_c in range(2):
                total = None
                for a in parity_taps[even_d]:
                    for b in parity_taps[even_r]:
                        for c in parity_taps[even_c]:
                            total = shifted[a, b, c] if total is None else total + shifted[a, b, c]
                col_parts.append(total)
            row_parts.append(jnp.stack(col_parts, -1))
        row_parts = jnp.stack(row_parts, 3)
        depth_parts.append(row_parts)
    joined = jnp.stack(depth_parts, 1)
    return joined.reshape(2 * depth, chans, 2 * rows, 2 * cols)


def activation_grad(preact, error):
    sigma = jax.nn.sigmoid(preact)
    return (error * (sigma * (1.0 + preact * (1.0 - sigma)))).astype(jnp.bfloat16)


def on_device(volume, weights, out_error):
    member = lax.axis_index("filt")
    tile = out_error.shape[1]
    below = shifted_2(volume[-1:], "slab", 1)
    extended = jnp.concatenate([below, volume], 0)
    whole = lax.all_gather(extended, "filt", axis=1, tiled=True)
    pieces = tap_pieces(whole, 1)
    kernel_tile = lax.dynamic_slice_in_dim(weights, member * tile, tile, 4)
    preact = forward_taps(pieces, kernel_tile)
    grad = activation_grad(preact, out_error)
    weight_part = weight_taps(pieces, grad)
    grad_rows = lax.all_to_all(grad, "filt", split_axis=2, concat_axis=1, tiled=True)
    count = out_error.shape[0] * lax.axis_size("slab") * out_error.shape[2] * out_error.shape[3]
    weight_grad = lax.psum(weight_part, "slab") * (1.0 / math.sqrt(count))
    upper = shifted_2(grad_rows, "slab", -1)
    grad_ext = jnp.concatenate([grad_rows, upper], 0)
    right_row = shifted_2(grad_ext, "filt", -1)
    grad_ext = jnp.concatenate([grad_ext, right_row], 2)
    in_grad = input_taps(grad_ext, weights).astype(jnp.bfloat16)
    return (in_grad, weight_grad)


def solution(mesh):
    in_specs = (P("slab", "filt", None, None), P(), P("slab", "filt", None, None))
    out_specs = (P("slab", None, "filt", None), P(None, None, None, None, "filt"))
    return jax.shard_map(
        on_device, mesh=mesh, in_specs=in_specs, out_specs=out_specs, check_vma=False
    )
```

profile of v0, /device:TPU:1, one launch (start us, length us, event | category | flops | bytes accessed | tf_op | source)
XLA Modules:
  0.0 422.1 jit_solution(12113445541933201036)
XLA Ops:
  8.1 5.4 %collective-permute-start = (bf16[1,16,16,256]{3,2,1,0:T(8,128)(2,1)S(1)}, bf16[1,16,16,256]{3,2,1,0:T(8,128)(2,1)S(1)}, u32[]{:S(2)}, u32[]{:S(2)}) collective-permute-start(bf16[1,16,16,256]{3,2,1,0:T(8,128)(2,1)S(1)} %slice.347), channel_id=1, source_target_pairs={{0,8},{8,16},{16,24},{24,32},{32,40},{40,48},{48,56},{56,64},{64,7... | collective-permute-start | bytes 393224 | tf_op jit(solution)/shard_map/ppermute | solution.py:11
  13.5 3.6 collective-permute-done
  17.1 1.7 pad_maximum_fusion
  18.9 51.0 %all-gather.2.cloned.1.call-done = bf16[3,128,16,256]{3,2,1,0:T(8,128)(2,1)} async-done(((bf16[3,16,16,256]{3,2,1,0:T(8,128)(2,1)}), bf16[3,128,16,256]{3,2,1,0:T(8,128)(2,1)}) %all-gather.2.cloned.1.call-update) | async-done | bytes 3145744 | tf_op jit(solution)/shard_map/all_gather | solution.py:104
  69.9 6.1 %copy.203 = bf16[3,128,16,256]{1,0,3,2:T(4,128)(2,1)} copy(bf16[3,128,16,256]{3,2,1,0:T(8,128)(2,1)} %all-gather.2.cloned.1.call-done) | data formatting | bytes 6291456
  76.0 3.9 pad.32.clone
  79.9 4.1 fusion.214
  84.0 11.3 %fusion.213 = (bf16[1,1,128,8,1,128,1]{2,1,0,6,5,4,3:T(2,128)(2,1)}, bf16[1,1,128,8,1,128,1]{2,1,0,6,5,4,3:T(2,128)(2,1)}, bf16[1,1,128,8,1,128,1]{2,1,0,6,5,4,3...) fusion(bf16[2,2,128,9,2,129,2]{2,1,0,6,5,4,3:T(2,128)(2,1)S(1)}, ...), kind=kLoop, calls=%fused_computation.343 | loop fusion | bytes 9961472 | tf_op jit(solution)/shard_map/slice | solution.py:25
  97.4 1.9 copy.158
  99.3 1.9 copy.156
  101.2 1.9 copy.154
  103.0 1.9 copy.152
  104.9 1.9 copy.150
  106.8 1.9 copy.202
  118.8 1.9 copy.180
  120.7 1.9 copy.178
  122.6 1.9 copy.176
  124.5 1.9 copy.174
  126.3 1.9 copy.172
  128.2 1.9 copy.170
  130.1 1.9 copy.168
  132.0 1.9 copy.166
  162.3 1.7 fusion.83
  164.0 1.6 fusion.27
  165.6 4.6 %all-to-all-start = ((bf16[1,32,8,128]{3,1,0,2:T(8,128)(2,1)}), bf16[1,32,8,128]{3,1,0,2:T(8,128)(2,1)S(1)}, u32[]{:S(2)}, u32[]{:S(2)}) async-start(bf16[1,32,8,128]{3,1,0,2:T(8,128)(2,1)} %bitcast.83), calls=%async_computation | async-start | bytes 131072 | tf_op jit(solution)/shard_map/all_to_all | solution.py:110
  170.5 1.8 fusion.26
  172.4 1.8 fusion.25
  174.2 1.8 fusion.24
  176.0 1.8 fusion.23
  177.8 1.7 fusion.22
  182.7 1.6 fusion.19
  184.4 1.6 fusion.18
  186.0 1.6 fusion.17
  187.7 1.6 fusion.16
  189.3 1.6 fusion.15
  191.0 1.6 fusion.14
  192.6 1.6 fusion.13
  194.3 1.6 fusion.12
  195.9 1.7 fusion.11
  197.6 1.6 fusion.10
  199.2 1.6 fusion.9
  200.9 1.6 fusion.8
  204.2 1.6 fusion.6
  207.5 1.8 fusion.4
  214.3 3.0 collective-permute-start.1
  217.3 3.2 collective-permute-done.1
  221.8 183.9 %all-reduce.12.cloned.1.call-done = f32[3,3,3,128,32]{3,4,2,1,0:T(8,128)} async-done(((f32[3,3,3,128,32]{3,4,2,1,0:T(8,128)}), f32[3,3,3,128,32]{3,4,2,1,0:T(8,128)}) %all-reduce.12.cloned.1.call-update) | async-done | bytes 442384 | tf_op jit(solution)/shard_map/psum | solution.py:112
  405.7 1.8 broadcast_multiply_fusion
  (151 shorter events, 61.8 us)
Async XLA Ops:
  7.2 62.7 %all-gather.2.cloned.1.call-start = ((), (), s32[]{:S(2)}) async-start(), calls=%async_computation.1 | async-start | bytes 3538944 | tf_op jit(solution)/shard_map/all_gather | solution.py:104
  8.1 9.0 %collective-permute-start = (bf16[1,16,16,256]{3,2,1,0:T(8,128)(2,1)S(1)}, bf16[1,16,16,256]{3,2,1,0:T(8,128)(2,1)S(1)}, u32[]{:S(2)}, u32[]{:S(2)}) collective-permute-start(bf16[1,16,16,256]{3,2,1,0:T(8,128)(2,1)S(1)} %slice.347), channel_id=1, source_target_pairs={{0,8},{8,16},{16,24},{24,32},{32,40},{40,48},{48,56},{56,64},{64,7... | collective-permute-start | bytes 393224 | tf_op jit(solution)/shard_map/ppermute | solution.py:11
  133.8 5.1 %copy-start = (bf16[1,1,128,8,1,128,1]{5,2,3,6,4,1,0:T(8,128)(2,1)S(1)}, bf16[1,1,128,8,1,128,1]{5,2,3,6,4,1,0:T(8,128)(2,1)}, u32[]{:S(2)}) copy-start(bf16[1,1,128,8,1,128,1]{5,2,3,6,4,1,0:T(8,128)(2,1)} %copy.158) | copy-start | bytes 786436
  136.4 7.0 %copy-start.16 = (bf16[1,1,128,8,1,128,1]{5,2,3,6,4,1,0:T(8,128)(2,1)S(1)}, bf16[1,1,128,8,1,128,1]{5,2,3,6,4,1,0:T(8,128)(2,1)}, u32[]{:S(2)}) copy-start(bf16[1,1,128,8,1,128,1]{5,2,3,6,4,1,0:T(8,128)(2,1)} %copy.166) | copy-start | bytes 786436
  137.7 6.8 %copy-start.14 = (bf16[1,1,128,8,1,128,1]{5,2,3,6,4,1,0:T(8,128)(2,1)S(1)}, bf16[1,1,128,8,1,128,1]{5,2,3,6,4,1,0:T(8,128)(2,1)}, u32[]{:S(2)}) copy-start(bf16[1,1,128,8,1,128,1]{5,2,3,6,4,1,0:T(8,128)(2,1)} %copy.168) | copy-start | bytes 786436
  139.0 6.5 %copy-start.11 = (bf16[1,1,128,8,1,128,1]{5,2,3,6,4,1,0:T(8,128)(2,1)S(1)}, bf16[1,1,128,8,1,128,1]{5,2,3,6,4,1,0:T(8,128)(2,1)}, u32[]{:S(2)}) copy-start(bf16[1,1,128,8,1,128,1]{5,2,3,6,4,1,0:T(8,128)(2,1)} %copy.170) | copy-start | bytes 786436
  140.1 6.5 %copy-start.9 = (bf16[1,1,128,8,1,128,1]{5,2,3,6,4,1,0:T(8,128)(2,1)S(1)}, bf16[1,1,128,8,1,128,1]{5,2,3,6,4,1,0:T(8,128)(2,1)}, u32[]{:S(2)}) copy-start(bf16[1,1,128,8,1,128,1]{5,2,3,6,4,1,0:T(8,128)(2,1)} %copy.172) | copy-start | bytes 786436
  141.1 6.5 %copy-start.7 = (bf16[1,1,128,8,1,128,1]{5,2,3,6,4,1,0:T(8,128)(2,1)S(1)}, bf16[1,1,128,8,1,128,1]{5,2,3,6,4,1,0:T(8,128)(2,1)}, u32[]{:S(2)}) copy-start(bf16[1,1,128,8,1,128,1]{5,2,3,6,4,1,0:T(8,128)(2,1)} %copy.174) | copy-start | bytes 786436
  142.2 6.4 %copy-start.5 = (bf16[1,1,128,8,1,128,1]{5,2,3,6,4,1,0:T(8,128)(2,1)S(1)}, bf16[1,1,128,8,1,128,1]{5,2,3,6,4,1,0:T(8,128)(2,1)}, u32[]{:S(2)}) copy-start(bf16[1,1,128,8,1,128,1]{5,2,3,6,4,1,0:T(8,128)(2,1)} %copy.176) | copy-start | bytes 786436
  143.3 6.4 %copy-start.3 = (bf16[1,1,128,8,1,128,1]{5,2,3,6,4,1,0:T(8,128)(2,1)S(1)}, bf16[1,1,128,8,1,128,1]{5,2,3,6,4,1,0:T(8,128)(2,1)}, u32[]{:S(2)}) copy-start(bf16[1,1,128,8,1,128,1]{5,2,3,6,4,1,0:T(8,128)(2,1)} %copy.178) | copy-start | bytes 786436
  144.4 6.3 %copy-start.1 = (bf16[1,1,128,8,1,128,1]{5,2,3,6,4,1,0:T(8,128)(2,1)S(1)}, bf16[1,1,128,8,1,128,1]{5,2,3,6,4,1,0:T(8,128)(2,1)}, u32[]{:S(2)}) copy-start(bf16[1,1,128,8,1,128,1]{5,2,3,6,4,1,0:T(8,128)(2,1)} %copy.180) | copy-start | bytes 786436
  155.9 6.3 %copy-start.18 = (bf16[1,1,128,8,1,128,1]{5,2,3,6,4,1,0:T(8,128)(2,1)S(1)}, bf16[1,1,128,8,1,128,1]{5,2,3,6,4,1,0:T(8,128)(2,1)}, u32[]{:S(2)}) copy-start(bf16[1,1,128,8,1,128,1]{5,2,3,6,4,1,0:T(8,128)(2,1)} %copy.202) | copy-start | bytes 786436
  155.9 6.3 %copy-start.21 = (bf16[1,32,8,128]{3,2,1,0:T(8,128)(2,1)S(1)}, bf16[1,32,8,128]{3,2,1,0:T(8,128)(2,1)}, u32[]{:S(2)}) copy-start(bf16[1,32,8,128]{3,2,1,0:T(8,128)(2,1)} %param.5) | copy-start | bytes 196612
  157.0 7.0 %copy-start.13 = (bf16[1,1,128,8,1,128,1]{5,2,3,6,4,1,0:T(8,128)(2,1)S(1)}, bf16[1,1,128,8,1,128,1]{5,2,3,6,4,1,0:T(8,128)(2,1)}, u32[]{:S(2)}) copy-start(bf16[1,1,128,8,1,128,1]{5,2,3,6,4,1,0:T(8,128)(2,1)} %copy.150) | copy-start | bytes 786436
  165.6 48.6 %all-to-all-start = ((bf16[1,32,8,128]{3,1,0,2:T(8,128)(2,1)}), bf16[1,32,8,128]{3,1,0,2:T(8,128)(2,1)S(1)}, u32[]{:S(2)}, u32[]{:S(2)}) async-start(bf16[1,32,8,128]{3,1,0,2:T(8,128)(2,1)} %bitcast.83), calls=%async_computation | async-start | bytes 131072 | tf_op jit(solution)/shard_map/all_to_all | solution.py:110
  170.3 235.4 %all-reduce.12.cloned.1.call-start = ((), (), s32[]{:S(2)}) async-start(), calls=%async_computation.2 | async-start | bytes 884736 | tf_op jit(solution)/shard_map/psum | solution.py:112
  170.5 12.3 %copy-start.17 = (bf16[1,1,128,8,1,128,1]{5,2,3,6,4,1,0:T(8,128)(2,1)S(1)}, bf16[1,1,128,8,1,128,1]{5,2,3,6,4,1,0:T(8,128)(2,1)}, u32[]{:S(2)}) copy-start(bf16[1,1,128,8,1,128,1]{5,2,3,6,4,1,0:T(8,128)(2,1)} %copy.166) | copy-start | bytes 786436
  170.5 13.9 %copy-start.15 = (bf16[1,1,128,8,1,128,1]{5,2,3,6,4,1,0:T(8,128)(2,1)S(1)}, bf16[1,1,128,8,1,128,1]{5,2,3,6,4,1,0:T(8,128)(2,1)}, u32[]{:S(2)}) copy-start(bf16[1,1,128,8,1,128,1]{5,2,3,6,4,1,0:T(8,128)(2,1)} %copy.168) | copy-start | bytes 786436
  170.5 15.5 %copy-start.12 = (bf16[1,1,128,8,1,128,1]{5,2,3,6,4,1,0:T(8,128)(2,1)S(1)}, bf16[1,1,128,8,1,128,1]{5,2,3,6,4,1,0:T(8,128)(2,1)}, u32[]{:S(2)}) copy-start(bf16[1,1,128,8,1,128,1]{5,2,3,6,4,1,0:T(8,128)(2,1)} %copy.170) | copy-start | bytes 786436
  170.5 17.2 %copy-start.10 = (bf16[1,1,128,8,1,128,1]{5,2,3,6,4,1,0:T(8,128)(2,1)S(1)}, bf16[1,1,128,8,1,128,1]{5,2,3,6,4,1,0:T(8,128)(2,1)}, u32[]{:S(2)}) copy-start(bf16[1,1,128,8,1,128,1]{5,2,3,6,4,1,0:T(8,128)(2,1)} %copy.172) | copy-start | bytes 786436
  172.4 17.0 %copy-start.8 = (bf16[1,1,128,8,1,128,1]{5,2,3,6,4,1,0:T(8,128)(2,1)S(1)}, bf16[1,1,128,8,1,128,1]{5,2,3,6,4,1,0:T(8,128)(2,1)}, u32[]{:S(2)}) copy-start(bf16[1,1,128,8,1,128,1]{5,2,3,6,4,1,0:T(8,128)(2,1)} %copy.174) | copy-start | bytes 786436
  174.2 16.8 %copy-start.6 = (bf16[1,1,128,8,1,128,1]{5,2,3,6,4,1,0:T(8,128)(2,1)S(1)}, bf16[1,1,128,8,1,128,1]{5,2,3,6,4,1,0:T(8,128)(2,1)}, u32[]{:S(2)}) copy-start(bf16[1,1,128,8,1,128,1]{5,2,3,6,4,1,0:T(8,128)(2,1)} %copy.176) | copy-start | bytes 786436
  176.0 16.7 %copy-start.4 = (bf16[1,1,128,8,1,128,1]{5,2,3,6,4,1,0:T(8,128)(2,1)S(1)}, bf16[1,1,128,8,1,128,1]{5,2,3,6,4,1,0:T(8,128)(2,1)}, u32[]{:S(2)}) copy-start(bf16[1,1,128,8,1,128,1]{5,2,3,6,4,1,0:T(8,128)(2,1)} %copy.178) | copy-start | bytes 786436
  177.8 16.5 %copy-start.2 = (bf16[1,1,128,8,1,128,1]{5,2,3,6,4,1,0:T(8,128)(2,1)S(1)}, bf16[1,1,128,8,1,128,1]{5,2,3,6,4,1,0:T(8,128)(2,1)}, u32[]{:S(2)}) copy-start(bf16[1,1,128,8,1,128,1]{5,2,3,6,4,1,0:T(8,128)(2,1)} %copy.180) | copy-start | bytes 786436
  195.9 16.6 %copy-start.19 = (bf16[1,1,128,8,1,128,1]{5,2,3,6,4,1,0:T(8,128)(2,1)S(1)}, bf16[1,1,128,8,1,128,1]{5,2,3,6,4,1,0:T(8,128)(2,1)}, u32[]{:S(2)}) copy-start(bf16[1,1,128,8,1,128,1]{5,2,3,6,4,1,0:T(8,128)(2,1)} %copy.202) | copy-start | bytes 786436
  207.5 200.0 %copy-start.20 = (bf16[3,3,3,128,256]{4,3,2,1,0:T(8,128)(2,1)S(1)}, bf16[3,3,3,128,256]{4,3,2,1,0:T(8,128)(2,1)}, u32[]{:S(2)}) copy-start(bf16[3,3,3,128,256]{4,3,2,1,0:T(8,128)(2,1)} %param.4) | copy-start | bytes 5308420
  214.3 6.1 %collective-permute-start.1 = (bf16[1,256,1,128]{1,3,2,0:T(8,128)(2,1)S(1)}, bf16[1,256,1,128]{1,3,2,0:T(8,128)(2,1)S(1)}, u32[]{:S(2)}, u32[]{:S(2)}) collective-permute-start(bf16[1,256,1,128]{1,3,2,0:T(8,128)(2,1)S(1)} %copy.115), channel_id=1, source_target_pairs={{8,0},{16,8},{24,16},{32,24},{40,32},{48,40},{56,48},{64,56},{72,6... | collective-permute-start | bytes 196616 | tf_op jit(solution)/shard_map/ppermute | solution.py:11
  220.5 187.0 %collective-permute-start.2 = (bf16[2,256,1,128]{1,3,2,0:T(8,128)(2,1)S(1)}, bf16[2,256,1,128]{1,3,2,0:T(8,128)(2,1)S(1)}, u32[]{:S(2)}, u32[]{:S(2)}) collective-permute-start(bf16[2,256,1,128]{1,3,2,0:T(8,128)(2,1)S(1)} %pad_maximum_fusion.2), channel_id=1, source_target_pairs={{1,0},{2,1},{3,2},{4,3},{5,4},{6,5},{7,6},{9,8},{10,9},{11,10},{12... | collective-permute-start | bytes 393224 | tf_op jit(solution)/shard_map/ppermute | solution.py:11
Sparse Core Ops, SparseCore 0:
  19.0 50.8 all-gather.1
  214.3 191.2 all-reduce.11
where the time goes:
time: 425 us; the launch traced here: 422 us
  waiting for transfers between devices  242 us (57%)
  matrix products  80.7 us (19%)
  local copies, waits for them, and re-layouts  66.4 us (16%)
  between operations  15 us (4%)
  starting transfers between devices  14.5 us (3%)
    psum x1, waiting for transfers between devices, on_device(): weight_grad = lax.psum(weight_part, 'slab') * (1.0 / math.sqrt(count))  184 us
    all_gather x1, waiting for transfers between devices, on_device(): whole = lax.all_gather(extended, 'filt', axis=1, tiled=True)  51 us
    unnamed x73, local copies, waits for them, and re-layouts  45.6 us
    dot_general x27, matrix products, weight_taps(): jnp.einsum('dkhw,dfhw->kf', piece, grad, preferred_element_type=jnp.float32)  45.2 us
    dot_general x27, matrix products, forward_taps(): jnp.einsum('dkhw,kf->dfhw', piece, kernel[a, b, c], preferred_element_typ...  29.6 us
    slice x2, local copies, waits for them, and re-layouts, tap_pieces(): split[a // 2:a // 2 + depth, a % 2, :, b // 2:b // 2 + rows, b % 2, c //...  15.4 us
    ppermute x3, starting transfers between devices, shifted_2(): lax.ppermute(value, axis, [(source, source + steps) for source in range(f...  9.64 us
  transfers between devices with their start and end apart: 6, of which 4 were waited for; matrix products, arithmetic and copies ran while one was open for 11% of the time, Pallas kernels for 0%

commit v1 on v0

--- a/solution.py
+++ b/solution.py
@@ -101,7 +101,9 @@
     tile = out_error.shape[1]
     below = shifted_2(volume[-1:], "slab", 1)
     extended = jnp.concatenate([below, volume], 0)
-    whole = lax.all_gather(extended, "filt", axis=1, tiled=True)
+    whole = jnp.concatenate(
+        lax.all_to_all(jnp.stack([extended] * lax.axis_size("filt")), "filt", 0, 0), axis=1
+    )
     pieces = tap_pieces(whole, 1)
     kernel_tile = lax.dynamic_slice_in_dim(weights, member * tile, tile, 4)
     preact = forward_taps(pieces, kernel_tile)

time: 425 us -> 456 us (1.073)
  waiting for transfers between devices: 242 us -> 267 us
    all_to_all x0 -> x1, waiting for transfers between devices: none -> 74.2 us  [on_device(): lax.all_to_all(jnp.stack([extended] * lax.axis_size('filt')), 'filt', 0, 0)]
    all_gather x1 -> x0, waiting for transfers between devices: 51 us -> none  [on_device(): whole = lax.all_gather(extended, 'filt', axis=1, tiled=True)]
    all_to_all x0 -> x1, starting transfers between devices: none -> 5.15 us  [on_device(): lax.all_to_all(jnp.stack([extended] * lax.axis_size('filt')), 'filt', 0, 0)]
  transfers between devices with their start and end apart: 6 -> 6, of which waited for: 4 -> 4; matrix products, arithmetic and copies ran while one was open for 11% -> 10% of each run, Pallas kernels for 0% -> 0%
where the time goes in v1:
time: 456 us; the launch traced here: 452 us
  waiting for transfers between devices  267 us (59%)
  matrix products  80.7 us (18%)
  local copies, waits for them, and re-layouts  68.8 us (15%)
  starting transfers between devices  17.7 us (4%)
  between operations  15 us (3%)
    psum x1, waiting for transfers between devices, on_device(): weight_grad = lax.psum(weight_part, 'slab') * (1.0 / math.sqrt(count))  185 us
    all_to_all x1, waiting for transfers between devices, on_device(): lax.all_to_all(jnp.stack([extended] * lax.axis_size('filt')), 'filt', 0, 0)  74.2 us
    dot_general x27, matrix products, weight_taps(): jnp.einsum('dkhw,dfhw->kf', piece, grad, preferred_element_type=jnp.float32)  45.2 us
    unnamed x73, local copies, waits for them, and re-layouts  43.9 us
    dot_general x27, matrix products, forward_taps(): jnp.einsum('dkhw,kf->dfhw', piece, kernel[a, b, c], preferred_element_typ...  29.6 us
    slice x2, local copies, waits for them, and re-layouts, tap_pieces(): split[a // 2:a // 2 + depth, a % 2, :, b // 2:b // 2 + rows, b % 2, c //...  15.4 us
  transfers between devices with their start and end apart: 6, of which 4 were waited for; matrix products, arithmetic and copies ran while one was open for 10% of the time, Pallas kernels for 0%

profile of v1, /device:TPU:1, one launch (start us, length us, event | category | flops | bytes accessed | tf_op | source)
XLA Modules:
  0.0 452.5 jit_solution(12254983364456366161)
XLA Ops:
  8.1 5.4 %collective-permute-start = (bf16[1,16,16,256]{3,2,1,0:T(8,128)(2,1)S(1)}, bf16[1,16,16,256]{3,2,1,0:T(8,128)(2,1)S(1)}, u32[]{:S(2)}, u32[]{:S(2)}) collective-permute-start(bf16[1,16,16,256]{3,2,1,0:T(8,128)(2,1)S(1)} %slice.347), channel_id=1, source_target_pairs={{0,8},{8,16},{16,24},{24,32},{32,40},{40,48},{48,56},{56,64},{64,7... | collective-permute-start | bytes 393224 | tf_op jit(solution)/shard_map/ppermute | solution.py:11
  13.5 3.6 collective-permute-done
  18.1 2.0 stack.166
  20.1 5.1 %all-to-all-start = ((bf16[8,3,16,16,256]{4,3,2,1,0:T(8,128)(2,1)}), bf16[8,3,16,16,256]{4,3,2,1,0:T(8,128)(2,1)}, u32[]{:S(2)}, u32[]{:S(2)}) async-start(bf16[8,3,16,16,256]{4,3,2,1,0:T(8,128)(2,1)} %stack.166), calls=%async_computation | async-start | bytes 6291456 | tf_op jit(solution)/shard_map/all_to_all | solution.py:105
  25.3 74.2 %all-to-all-done = bf16[8,3,16,16,256]{4,3,2,1,0:T(8,128)(2,1)} async-done(((bf16[8,3,16,16,256]{4,3,2,1,0:T(8,128)(2,1)}), bf16[8,3,16,16,256]{4,3,2,1,0:T(8,128)(2,1)}, u32[]{:S(2)}, u32[]{:S(2)}) %all-to-all-start) | async-done | bytes 3145760 | tf_op jit(solution)/shard_map/all_to_all | solution.py:105
  99.5 2.2 copy.86
  101.7 4.3 copy.205
  106.0 3.9 pad.32.clone
  109.9 4.1 fusion.214
  114.0 11.3 %fusion.213 = (bf16[1,1,128,8,1,128,1]{2,1,0,6,5,4,3:T(2,128)(2,1)}, bf16[1,1,128,8,1,128,1]{2,1,0,6,5,4,3:T(2,128)(2,1)}, bf16[1,1,128,8,1,128,1]{2,1,0,6,5,4,3...) fusion(bf16[2,2,128,9,2,129,2]{2,1,0,6,5,4,3:T(2,128)(2,1)S(1)}, ...), kind=kLoop, calls=%fused_computation.343 | loop fusion | bytes 9961472 | tf_op jit(solution)/shard_map/slice | solution.py:25
  127.4 1.9 copy.160
  129.3 1.9 copy.158
  131.2 1.9 copy.156
  133.0 1.9 copy.154
  134.9 1.9 copy.152
  136.8 1.9 copy.204
  148.8 1.9 copy.182
  150.7 1.9 copy.180
  152.6 1.9 copy.178
  154.5 1.9 copy.176
  156.3 1.9 copy.174
  158.2 1.9 copy.172
  160.1 1.9 copy.170
  162.0 1.9 copy.168
  192.3 1.7 fusion.83
  194.0 1.6 fusion.27
  195.7 3.5 all-to-all-start.1
  199.3 1.8 fusion.26
  201.1 1.8 fusion.25
  202.9 1.8 fusion.24
  204.7 1.8 fusion.23
  206.5 1.7 fusion.22
  211.5 1.6 fusion.19
  213.2 1.6 fusion.18
  214.8 1.6 fusion.17
  216.4 1.6 fusion.16
  218.1 1.6 fusion.15
  221.4 1.6 fusion.13
  223.0 1.6 fusion.12
  224.7 1.7 fusion.11
  228.0 1.6 fusion.9
  231.3 1.6 fusion.7
  236.2 1.8 fusion.4
  238.0 1.6 fusion.3
  243.1 2.3 collective-permute-start.1
  245.4 4.1 collective-permute-done.1
  250.8 185.2 %all-reduce.12.cloned.1.call-done = f32[3,3,3,128,32]{3,4,2,1,0:T(8,128)} async-done(((f32[3,3,3,128,32]{3,4,2,1,0:T(8,128)}), f32[3,3,3,128,32]{3,4,2,1,0:T(8,128)}) %all-reduce.12.cloned.1.call-update) | async-done | bytes 442384 | tf_op jit(solution)/shard_map/psum | solution.py:114
  436.0 1.8 broadcast_multiply_fusion
  (152 shorter events, 65.8 us)
Async XLA Ops:
  8.1 9.0 %collective-permute-start = (bf16[1,16,16,256]{3,2,1,0:T(8,128)(2,1)S(1)}, bf16[1,16,16,256]{3,2,1,0:T(8,128)(2,1)S(1)}, u32[]{:S(2)}, u32[]{:S(2)}) collective-permute-start(bf16[1,16,16,256]{3,2,1,0:T(8,128)(2,1)S(1)} %slice.347), channel_id=1, source_target_pairs={{0,8},{8,16},{16,24},{24,32},{32,40},{40,48},{48,56},{56,64},{64,7... | collective-permute-start | bytes 393224 | tf_op jit(solution)/shard_map/ppermute | solution.py:11
  20.1 79.4 %all-to-all-start = ((bf16[8,3,16,16,256]{4,3,2,1,0:T(8,128)(2,1)}), bf16[8,3,16,16,256]{4,3,2,1,0:T(8,128)(2,1)}, u32[]{:S(2)}, u32[]{:S(2)}) async-start(bf16[8,3,16,16,256]{4,3,2,1,0:T(8,128)(2,1)} %stack.166), calls=%async_computation | async-start | bytes 6291456 | tf_op jit(solution)/shard_map/all_to_all | solution.py:105
  163.9 5.1 %copy-start = (bf16[1,1,128,8,1,128,1]{5,2,3,6,4,1,0:T(8,128)(2,1)S(1)}, bf16[1,1,128,8,1,128,1]{5,2,3,6,4,1,0:T(8,128)(2,1)}, u32[]{:S(2)}) copy-start(bf16[1,1,128,8,1,128,1]{5,2,3,6,4,1,0:T(8,128)(2,1)} %copy.160) | copy-start | bytes 786436
  166.4 7.0 %copy-start.16 = (bf16[1,1,128,8,1,128,1]{5,2,3,6,4,1,0:T(8,128)(2,1)S(1)}, bf16[1,1,128,8,1,128,1]{5,2,3,6,4,1,0:T(8,128)(2,1)}, u32[]{:S(2)}) copy-start(bf16[1,1,128,8,1,128,1]{5,2,3,6,4,1,0:T(8,128)(2,1)} %copy.168) | copy-start | bytes 786436
  167.7 6.8 %copy-start.14 = (bf16[1,1,128,8,1,128,1]{5,2,3,6,4,1,0:T(8,128)(2,1)S(1)}, bf16[1,1,128,8,1,128,1]{5,2,3,6,4,1,0:T(8,128)(2,1)}, u32[]{:S(2)}) copy-start(bf16[1,1,128,8,1,128,1]{5,2,3,6,4,1,0:T(8,128)(2,1)} %copy.170) | copy-start | bytes 786436
  169.0 6.5 %copy-start.11 = (bf16[1,1,128,8,1,128,1]{5,2,3,6,4,1,0:T(8,128)(2,1)S(1)}, bf16[1,1,128,8,1,128,1]{5,2,3,6,4,1,0:T(8,128)(2,1)}, u32[]{:S(2)}) copy-start(bf16[1,1,128,8,1,128,1]{5,2,3,6,4,1,0:T(8,128)(2,1)} %copy.172) | copy-start | bytes 786436
  170.1 6.5 %copy-start.9 = (bf16[1,1,128,8,1,128,1]{5,2,3,6,4,1,0:T(8,128)(2,1)S(1)}, bf16[1,1,128,8,1,128,1]{5,2,3,6,4,1,0:T(8,128)(2,1)}, u32[]{:S(2)}) copy-start(bf16[1,1,128,8,1,128,1]{5,2,3,6,4,1,0:T(8,128)(2,1)} %copy.174) | copy-start | bytes 786436
  171.2 6.5 %copy-start.7 = (bf16[1,1,128,8,1,128,1]{5,2,3,6,4,1,0:T(8,128)(2,1)S(1)}, bf16[1,1,128,8,1,128,1]{5,2,3,6,4,1,0:T(8,128)(2,1)}, u32[]{:S(2)}) copy-start(bf16[1,1,128,8,1,128,1]{5,2,3,6,4,1,0:T(8,128)(2,1)} %copy.176) | copy-start | bytes 786436
  172.3 6.4 %copy-start.5 = (bf16[1,1,128,8,1,128,1]{5,2,3,6,4,1,0:T(8,128)(2,1)S(1)}, bf16[1,1,128,8,1,128,1]{5,2,3,6,4,1,0:T(8,128)(2,1)}, u32[]{:S(2)}) copy-start(bf16[1,1,128,8,1,128,1]{5,2,3,6,4,1,0:T(8,128)(2,1)} %copy.178) | copy-start | bytes 786436
  173.4 6.4 %copy-start.3 = (bf16[1,1,128,8,1,128,1]{5,2,3,6,4,1,0:T(8,128)(2,1)S(1)}, bf16[1,1,128,8,1,128,1]{5,2,3,6,4,1,0:T(8,128)(2,1)}, u32[]{:S(2)}) copy-start(bf16[1,1,128,8,1,128,1]{5,2,3,6,4,1,0:T(8,128)(2,1)} %copy.180) | copy-start | bytes 786436
  174.5 6.3 %copy-start.1 = (bf16[1,1,128,8,1,128,1]{5,2,3,6,4,1,0:T(8,128)(2,1)S(1)}, bf16[1,1,128,8,1,128,1]{5,2,3,6,4,1,0:T(8,128)(2,1)}, u32[]{:S(2)}) copy-start(bf16[1,1,128,8,1,128,1]{5,2,3,6,4,1,0:T(8,128)(2,1)} %copy.182) | copy-start | bytes 786436
  186.0 6.3 %copy-start.18 = (bf16[1,1,128,8,1,128,1]{5,2,3,6,4,1,0:T(8,128)(2,1)S(1)}, bf16[1,1,128,8,1,128,1]{5,2,3,6,4,1,0:T(8,128)(2,1)}, u32[]{:S(2)}) copy-start(bf16[1,1,128,8,1,128,1]{5,2,3,6,4,1,0:T(8,128)(2,1)} %copy.204) | copy-start | bytes 786436
  186.0 6.3 %copy-start.21 = (bf16[1,32,8,128]{3,2,1,0:T(8,128)(2,1)S(1)}, bf16[1,32,8,128]{3,2,1,0:T(8,128)(2,1)}, u32[]{:S(2)}) copy-start(bf16[1,32,8,128]{3,2,1,0:T(8,128)(2,1)} %param.5) | copy-start | bytes 196612
  187.1 7.0 %copy-start.13 = (bf16[1,1,128,8,1,128,1]{5,2,3,6,4,1,0:T(8,128)(2,1)S(1)}, bf16[1,1,128,8,1,128,1]{5,2,3,6,4,1,0:T(8,128)(2,1)}, u32[]{:S(2)}) copy-start(bf16[1,1,128,8,1,128,1]{5,2,3,6,4,1,0:T(8,128)(2,1)} %copy.152) | copy-start | bytes 786436
  195.7 47.3 %all-to-all-start.1 = ((bf16[1,32,8,128]{3,1,0,2:T(8,128)(2,1)}), bf16[1,32,8,128]{3,1,0,2:T(8,128)(2,1)S(1)}, u32[]{:S(2)}, u32[]{:S(2)}) async-start(bf16[1,32,8,128]{3,1,0,2:T(8,128)(2,1)} %bitcast.85), calls=%async_computation.1 | async-start | bytes 131072 | tf_op jit(solution)/shard_map/all_to_all | solution.py:112
  199.2 236.8 %all-reduce.12.cloned.1.call-start = ((), (), s32[]{:S(2)}) async-start(), calls=%async_computation.2 | async-start | bytes 884736 | tf_op jit(solution)/shard_map/psum | solution.py:114
  199.2 12.3 %copy-start.17 = (bf16[1,1,128,8,1,128,1]{5,2,3,6,4,1,0:T(8,128)(2,1)S(1)}, bf16[1,1,128,8,1,128,1]{5,2,3,6,4,1,0:T(8,128)(2,1)}, u32[]{:S(2)}) copy-start(bf16[1,1,128,8,1,128,1]{5,2,3,6,4,1,0:T(8,128)(2,1)} %copy.168) | copy-start | bytes 786436
  199.3 13.9 %copy-start.15 = (bf16[1,1,128,8,1,128,1]{5,2,3,6,4,1,0:T(8,128)(2,1)S(1)}, bf16[1,1,128,8,1,128,1]{5,2,3,6,4,1,0:T(8,128)(2,1)}, u32[]{:S(2)}) copy-start(bf16[1,1,128,8,1,128,1]{5,2,3,6,4,1,0:T(8,128)(2,1)} %copy.170) | copy-start | bytes 786436
  199.3 15.5 %copy-start.12 = (bf16[1,1,128,8,1,128,1]{5,2,3,6,4,1,0:T(8,128)(2,1)S(1)}, bf16[1,1,128,8,1,128,1]{5,2,3,6,4,1,0:T(8,128)(2,1)}, u32[]{:S(2)}) copy-start(bf16[1,1,128,8,1,128,1]{5,2,3,6,4,1,0:T(8,128)(2,1)} %copy.172) | copy-start | bytes 786436
  199.3 17.2 %copy-start.10 = (bf16[1,1,128,8,1,128,1]{5,2,3,6,4,1,0:T(8,128)(2,1)S(1)}, bf16[1,1,128,8,1,128,1]{5,2,3,6,4,1,0:T(8,128)(2,1)}, u32[]{:S(2)}) copy-start(bf16[1,1,128,8,1,128,1]{5,2,3,6,4,1,0:T(8,128)(2,1)} %copy.174) | copy-start | bytes 786436
  201.1 17.0 %copy-start.8 = (bf16[1,1,128,8,1,128,1]{5,2,3,6,4,1,0:T(8,128)(2,1)S(1)}, bf16[1,1,128,8,1,128,1]{5,2,3,6,4,1,0:T(8,128)(2,1)}, u32[]{:S(2)}) copy-start(bf16[1,1,128,8,1,128,1]{5,2,3,6,4,1,0:T(8,128)(2,1)} %copy.176) | copy-start | bytes 786436
  202.9 16.8 %copy-start.6 = (bf16[1,1,128,8,1,128,1]{5,2,3,6,4,1,0:T(8,128)(2,1)S(1)}, bf16[1,1,128,8,1,128,1]{5,2,3,6,4,1,0:T(8,128)(2,1)}, u32[]{:S(2)}) copy-start(bf16[1,1,128,8,1,128,1]{5,2,3,6,4,1,0:T(8,128)(2,1)} %copy.178) | copy-start | bytes 786436
  204.7 16.7 %copy-start.4 = (bf16[1,1,128,8,1,128,1]{5,2,3,6,4,1,0:T(8,128)(2,1)S(1)}, bf16[1,1,128,8,1,128,1]{5,2,3,6,4,1,0:T(8,128)(2,1)}, u32[]{:S(2)}) copy-start(bf16[1,1,128,8,1,128,1]{5,2,3,6,4,1,0:T(8,128)(2,1)} %copy.180) | copy-start | bytes 786436
  206.5 16.5 %copy-start.2 = (bf16[1,1,128,8,1,128,1]{5,2,3,6,4,1,0:T(8,128)(2,1)S(1)}, bf16[1,1,128,8,1,128,1]{5,2,3,6,4,1,0:T(8,128)(2,1)}, u32[]{:S(2)}) copy-start(bf16[1,1,128,8,1,128,1]{5,2,3,6,4,1,0:T(8,128)(2,1)} %copy.182) | copy-start | bytes 786436
  224.7 16.6 %copy-start.19 = (bf16[1,1,128,8,1,128,1]{5,2,3,6,4,1,0:T(8,128)(2,1)S(1)}, bf16[1,1,128,8,1,128,1]{5,2,3,6,4,1,0:T(8,128)(2,1)}, u32[]{:S(2)}) copy-start(bf16[1,1,128,8,1,128,1]{5,2,3,6,4,1,0:T(8,128)(2,1)} %copy.204) | copy-start | bytes 786436
  236.2 201.6 %copy-start.20 = (bf16[3,3,3,128,256]{4,3,2,1,0:T(8,128)(2,1)S(1)}, bf16[3,3,3,128,256]{4,3,2,1,0:T(8,128)(2,1)}, u32[]{:S(2)}) copy-start(bf16[3,3,3,128,256]{4,3,2,1,0:T(8,128)(2,1)} %param.4) | copy-start | bytes 5308420
  243.1 6.4 %collective-permute-start.1 = (bf16[1,256,1,128]{1,3,2,0:T(8,128)(2,1)S(1)}, bf16[1,256,1,128]{1,3,2,0:T(8,128)(2,1)S(1)}, u32[]{:S(2)}, u32[]{:S(2)}) collective-permute-start(bf16[1,256,1,128]{1,3,2,0:T(8,128)(2,1)S(1)} %copy.117), channel_id=1, source_target_pairs={{8,0},{16,8},{24,16},{32,24},{40,32},{48,40},{56,48},{64,56},{72,6... | collective-permute-start | bytes 196616 | tf_op jit(solution)/shard_map/ppermute | solution.py:11
  249.5 188.3 %collective-permute-start.2 = (bf16[2,256,1,128]{1,3,2,0:T(8,128)(2,1)S(1)}, bf16[2,256,1,128]{1,3,2,0:T(8,128)(2,1)S(1)}, u32[]{:S(2)}, u32[]{:S(2)}) collective-permute-start(bf16[2,256,1,128]{1,3,2,0:T(8,128)(2,1)S(1)} %pad_maximum_fusion.2), channel_id=1, source_target_pairs={{1,0},{2,1},{3,2},{4,3},{5,4},{6,5},{7,6},{9,8},{10,9},{11,10},{12... | collective-permute-start | bytes 393224 | tf_op jit(solution)/shard_map/ppermute | solution.py:11
Sparse Core Ops, SparseCore 0:
  243.1 192.8 all-reduce.11
